TPU v7x, 256 devices: a whole 4x4x8 slice. The times are simulated.
256 devices in a mesh: row: 16 (over x_lo, z), col: 16 (over y, x_hi, core).
Axes of the slice: x: 4 (x_hi: 2, x_lo: 2; x = x_hi * 2 + x_lo), y: 4, z: 8, core: 2. Of those that a mesh axis runs over, the one named last changes fastest.
Arguments:
- features: bfloat16 [524288, 128], P(('col', 'row')), may hold values from -6 to 6
- weight: bfloat16 [128, 128], replicated, may hold values from -0.5 to 0.5
- tile_row: int32 [262144], P(('row', 'col')), may hold values from 0 to 255
- tile_col: int32 [262144], P(('row', 'col')), may hold values from 0 to 255
- tile_count: int32 [256], P(('row', 'col')), may hold values from 256 to 1024, as said below
- edge_row: int32 [262144, 64], P(('row', 'col')), may hold values from 0 to 127, as said below
- edge_col: int32 [262144, 64], P(('row', 'col')), may hold values from 0 to 127
- edge_weight: bfloat16 [262144, 64], P(('row', 'col')), may hold values from 0.049804688 to 0.5
Outputs:
- activated: bfloat16 [524288, 128], P(('row', 'col'))
Inputs may be any that keep to these rules, and one draw needn't show every extreme that they name: The first tile_count[d] slots of a device hold its nonzero tiles, at distinct positions and in increasing order of (tile_row, tile_col); exactly one device fills all 1024 slots; later slots are unused. `edge_row`: the 64 edges of a tile lie at distinct positions of the tile.
All inputs are finite; a program needn't handle non-finite values.
Results may differ from a plain program's by a relative error of at most 0.0049.
Values may be sent and summed in bfloat16 or wider, within the bound.
A program may use at most 128 MiB of HBM per device.

v0:
```python
import jax
import jax.numpy as jnp
from jax import lax
from jax.sharding import PartitionSpec as P

TILE = 128


def tile_products(
    accum,
    base,
    first_slot,
    last_slot,
    tile_row,
    tile_col,
    edge_row,
    edge_col,
    edge_weight,
    column_block,
):
    slot_total = tile_row.shape[0]
    block = 64
    side = accum.shape[1]
    width = column_block.shape[1]
    positions = jnp.arange(side, dtype=jnp.int32)

    def one_block(number, accum):
        begin = number * block
        rows = lax.dynamic_slice_in_dim(tile_row, begin, block, 0)
        cols = lax.dynamic_slice_in_dim(tile_col, begin, block, 0)
        erows = lax.dynamic_slice_in_dim(edge_row, begin, block, 0)
        ecols = lax.dynamic_slice_in_dim(edge_col, begin, block, 0)
        weights = lax.dynamic_slice_in_dim(edge_weight, begin, block, 0)
        slots = begin + jnp.arange(block, dtype=jnp.int32)
        valid = (slots >= first_slot) & (slots < last_slot)
        sources = (cols[:, None] * side + ecols).reshape(-1)
        gathered = column_block[sources].reshape(block, erows.shape[1], width)
        row_table = (positions[None, :, None] == erows[:, None, :]).astype(jnp.bfloat16) * weights[
            :, None, :
        ]
        product = jnp.einsum(
            "bte,bef->btf", row_table, gathered, preferred_element_type=jnp.float32
        )
        product = jnp.where(valid[:, None, None], product, jnp.float32(0.0))
        target = jnp.where(valid, rows - base, 0)
        return accum.at[target].add(product)

    return lax.fori_loop(first_slot // block, (last_slot + block - 1) // block, one_block, accum)


def local(features, weight, tile_row, tile_col, tile_count, edge_row, edge_col, edge_weight):
    node_rows = features.shape[0]
    width = weight.shape[1]
    transformed = jnp.dot(features, weight, preferred_element_type=jnp.float32).astype(jnp.bfloat16)
    column_block = lax.all_gather(transformed, "row", axis=0, tiled=True)
    block_rows = lax.axis_size("col") * node_rows
    tile_rows = block_rows // TILE
    live_count = tile_count[0]
    accum = jnp.zeros((tile_rows, TILE, width), jnp.float32)
    accum = tile_products(
        accum, 0, 0, live_count, tile_row, tile_col, edge_row, edge_col, edge_weight, column_block
    )
    summed = lax.psum_scatter(
        accum.reshape(block_rows, width), "col", scatter_dimension=0, tiled=True
    )
    return jnp.maximum(summed, jnp.float32(0.0)).astype(jnp.bfloat16)


def solution(mesh):
    in_specs = (
        P(("col", "row"), None),
        P(),
        P(("row", "col")),
        P(("row", "col")),
        P(("row", "col")),
        P(("row", "col"), None),
        P(("row", "col"), None),
        P(("row", "col"), None),
    )
    out_specs = P(("row", "col"), None)
    return jax.shard_map(local, mesh=mesh, in_specs=in_specs, out_specs=out_specs, check_vma=False)
```

profile of v0, /device:TPU:1, one launch (start us, length us, event | category | flops | bytes accessed | tf_op | source)
XLA Modules:
  0.0 867.1 jit_solution(10120300553230724459)
XLA Ops:
  10.1 104.2 %all-gather.2.cloned.1.call-done = bf16[32768,128]{1,0:T(8,128)(2,1)} async-done(((bf16[2048,128]{1,0:T(8,128)(2,1)}), bf16[32768,128]{1,0:T(8,128)(2,1)}) %all-gather.2.cloned.1.call-update) | async-done | bytes 8388624 | tf_op jit(solution)/shard_map/all_gather | solution.py:55
  122.2 584.5 %while.11 = (s32[]{:T(128)}, f32[256,128,128]{2,1,0:T(8,128)}, s32[]{:T(128)}, s32[]{:T(128)}, s32[1024]{0:T(1024)}, /*index=5*/s32[1024,64]{0,1:T(8,128)}, bf16...) while((s32[]{:T(128)}, f32[256,128,128]{2,1,0:T(8,128)}, ...), condition=%wide.region_2.3_spmd.clone, body=%wide.region_0.2_spmd.clone.sunk | while | flops 137384512 | bytes 20260680 | solution.py:48
  125.8 15.5 %gather_fusion = bf16[4096,128]{1,0:T(8,128)(2,1)S(1)} fusion(bf16[32768,128]{1,0:T(8,128)(2,1)} %get-tuple-element.241, s32[4096]{0:T(1024)S(1)} %broadcast_clamp_fusion.2), kind=kCustom, calls=%fused_computation.clone.clone.1 | custom fusion | bytes 2113536 | tf_op jit(solution)/shard_map/while/body/gather | solution.py:37
  145.7 13.1 %scatter_fusion = f32[256,128,128]{2,1,0:T(8,128)} fusion(f32[256,128,128]{2,1,0:T(8,128)} %get-tuple-element.219, s32[64]{0:T(128)S(1)} %get-tuple-element.199, f32[64,128,128]{2,1,0:T(8,128)} %convolution_select_fusion.2), kind=kCustom, calls=%fused_computation.1.clone.clone.1 | custom fusion | flops 1048576 | bytes 12583168 | tf_op jit(solution)/shard_map/while/body/scatter-add | solution.py:46
  162.4 15.5 %gather_fusion = bf16[4096,128]{1,0:T(8,128)(2,1)S(1)} fusion(bf16[32768,128]{1,0:T(8,128)(2,1)} %get-tuple-element.241, s32[4096]{0:T(1024)S(1)} %broadcast_clamp_fusion.2), kind=kCustom, calls=%fused_computation.clone.clone.1 | custom fusion | bytes 2113536 | tf_op jit(solution)/shard_map/while/body/gather | solution.py:37
  198.8 15.5 %gather_fusion = bf16[4096,128]{1,0:T(8,128)(2,1)S(1)} fusion(bf16[32768,128]{1,0:T(8,128)(2,1)} %get-tuple-element.241, s32[4096]{0:T(1024)S(1)} %broadcast_clamp_fusion.2), kind=kCustom, calls=%fused_computation.clone.clone.1 | custom fusion | bytes 2113536 | tf_op jit(solution)/shard_map/while/body/gather | solution.py:37
  235.3 15.5 %gather_fusion = bf16[4096,128]{1,0:T(8,128)(2,1)S(1)} fusion(bf16[32768,128]{1,0:T(8,128)(2,1)} %get-tuple-element.241, s32[4096]{0:T(1024)S(1)} %broadcast_clamp_fusion.2), kind=kCustom, calls=%fused_computation.clone.clone.1 | custom fusion | bytes 2113536 | tf_op jit(solution)/shard_map/while/body/gather | solution.py:37
  271.7 15.5 %gather_fusion = bf16[4096,128]{1,0:T(8,128)(2,1)S(1)} fusion(bf16[32768,128]{1,0:T(8,128)(2,1)} %get-tuple-element.241, s32[4096]{0:T(1024)S(1)} %broadcast_clamp_fusion.2), kind=kCustom, calls=%fused_computation.clone.clone.1 | custom fusion | bytes 2113536 | tf_op jit(solution)/shard_map/while/body/gather | solution.py:37
  308.1 15.5 %gather_fusion = bf16[4096,128]{1,0:T(8,128)(2,1)S(1)} fusion(bf16[32768,128]{1,0:T(8,128)(2,1)} %get-tuple-element.241, s32[4096]{0:T(1024)S(1)} %broadcast_clamp_fusion.2), kind=kCustom, calls=%fused_computation.clone.clone.1 | custom fusion | bytes 2113536 | tf_op jit(solution)/shard_map/while/body/gather | solution.py:37
  328.1 13.0 %scatter_fusion = f32[256,128,128]{2,1,0:T(8,128)} fusion(f32[256,128,128]{2,1,0:T(8,128)} %get-tuple-element.219, s32[64]{0:T(128)S(1)} %get-tuple-element.199, f32[64,128,128]{2,1,0:T(8,128)} %convolution_select_fusion.2), kind=kCustom, calls=%fused_computation.1.clone.clone.1 | custom fusion | flops 1048576 | bytes 12583168 | tf_op jit(solution)/shard_map/while/body/scatter-add | solution.py:46
  344.6 15.5 %gather_fusion = bf16[4096,128]{1,0:T(8,128)(2,1)S(1)} fusion(bf16[32768,128]{1,0:T(8,128)(2,1)} %get-tuple-element.241, s32[4096]{0:T(1024)S(1)} %broadcast_clamp_fusion.2), kind=kCustom, calls=%fused_computation.clone.clone.1 | custom fusion | bytes 2113536 | tf_op jit(solution)/shard_map/while/body/gather | solution.py:37
  381.1 15.5 %gather_fusion = bf16[4096,128]{1,0:T(8,128)(2,1)S(1)} fusion(bf16[32768,128]{1,0:T(8,128)(2,1)} %get-tuple-element.241, s32[4096]{0:T(1024)S(1)} %broadcast_clamp_fusion.2), kind=kCustom, calls=%fused_computation.clone.clone.1 | custom fusion | bytes 2113536 | tf_op jit(solution)/shard_map/while/body/gather | solution.py:37
  401.0 13.3 %scatter_fusion = f32[256,128,128]{2,1,0:T(8,128)} fusion(f32[256,128,128]{2,1,0:T(8,128)} %get-tuple-element.219, s32[64]{0:T(128)S(1)} %get-tuple-element.199, f32[64,128,128]{2,1,0:T(8,128)} %convolution_select_fusion.2), kind=kCustom, calls=%fused_computation.1.clone.clone.1 | custom fusion | flops 1048576 | bytes 12583168 | tf_op jit(solution)/shard_map/while/body/scatter-add | solution.py:46
  417.9 15.5 %gather_fusion = bf16[4096,128]{1,0:T(8,128)(2,1)S(1)} fusion(bf16[32768,128]{1,0:T(8,128)(2,1)} %get-tuple-element.241, s32[4096]{0:T(1024)S(1)} %broadcast_clamp_fusion.2), kind=kCustom, calls=%fused_computation.clone.clone.1 | custom fusion | bytes 2113536 | tf_op jit(solution)/shard_map/while/body/gather | solution.py:37
  437.8 13.0 %scatter_fusion = f32[256,128,128]{2,1,0:T(8,128)} fusion(f32[256,128,128]{2,1,0:T(8,128)} %get-tuple-element.219, s32[64]{0:T(128)S(1)} %get-tuple-element.199, f32[64,128,128]{2,1,0:T(8,128)} %convolution_select_fusion.2), kind=kCustom, calls=%fused_computation.1.clone.clone.1 | custom fusion | flops 1048576 | bytes 12583168 | tf_op jit(solution)/shard_map/while/body/scatter-add | solution.py:46
  454.4 15.5 %gather_fusion = bf16[4096,128]{1,0:T(8,128)(2,1)S(1)} fusion(bf16[32768,128]{1,0:T(8,128)(2,1)} %get-tuple-element.241, s32[4096]{0:T(1024)S(1)} %broadcast_clamp_fusion.2), kind=kCustom, calls=%fused_computation.clone.clone.1 | custom fusion | bytes 2113536 | tf_op jit(solution)/shard_map/while/body/gather | solution.py:37
  490.8 15.5 %gather_fusion = bf16[4096,128]{1,0:T(8,128)(2,1)S(1)} fusion(bf16[32768,128]{1,0:T(8,128)(2,1)} %get-tuple-element.241, s32[4096]{0:T(1024)S(1)} %broadcast_clamp_fusion.2), kind=kCustom, calls=%fused_computation.clone.clone.1 | custom fusion | bytes 2113536 | tf_op jit(solution)/shard_map/while/body/gather | solution.py:37
  527.3 15.5 %gather_fusion = bf16[4096,128]{1,0:T(8,128)(2,1)S(1)} fusion(bf16[32768,128]{1,0:T(8,128)(2,1)} %get-tuple-element.241, s32[4096]{0:T(1024)S(1)} %broadcast_clamp_fusion.2), kind=kCustom, calls=%fused_computation.clone.clone.1 | custom fusion | bytes 2113536 | tf_op jit(solution)/shard_map/while/body/gather | solution.py:37
  563.7 15.5 %gather_fusion = bf16[4096,128]{1,0:T(8,128)(2,1)S(1)} fusion(bf16[32768,128]{1,0:T(8,128)(2,1)} %get-tuple-element.241, s32[4096]{0:T(1024)S(1)} %broadcast_clamp_fusion.2), kind=kCustom, calls=%fused_computation.clone.clone.1 | custom fusion | bytes 2113536 | tf_op jit(solution)/shard_map/while/body/gather | solution.py:37
  600.2 15.5 %gather_fusion = bf16[4096,128]{1,0:T(8,128)(2,1)S(1)} fusion(bf16[32768,128]{1,0:T(8,128)(2,1)} %get-tuple-element.241, s32[4096]{0:T(1024)S(1)} %broadcast_clamp_fusion.2), kind=kCustom, calls=%fused_computation.clone.clone.1 | custom fusion | bytes 2113536 | tf_op jit(solution)/shard_map/while/body/gather | solution.py:37
  636.7 15.5 %gather_fusion = bf16[4096,128]{1,0:T(8,128)(2,1)S(1)} fusion(bf16[32768,128]{1,0:T(8,128)(2,1)} %get-tuple-element.241, s32[4096]{0:T(1024)S(1)} %broadcast_clamp_fusion.2), kind=kCustom, calls=%fused_computation.clone.clone.1 | custom fusion | bytes 2113536 | tf_op jit(solution)/shard_map/while/body/gather | solution.py:37
  673.1 15.5 %gather_fusion = bf16[4096,128]{1,0:T(8,128)(2,1)S(1)} fusion(bf16[32768,128]{1,0:T(8,128)(2,1)} %get-tuple-element.241, s32[4096]{0:T(1024)S(1)} %broadcast_clamp_fusion.2), kind=kCustom, calls=%fused_computation.clone.clone.1 | custom fusion | bytes 2113536 | tf_op jit(solution)/shard_map/while/body/gather | solution.py:37
  693.1 13.7 %scatter_fusion = f32[256,128,128]{2,1,0:T(8,128)} fusion(f32[256,128,128]{2,1,0:T(8,128)} %get-tuple-element.219, s32[64]{0:T(128)S(1)} %get-tuple-element.199, f32[64,128,128]{2,1,0:T(8,128)} %convolution_select_fusion.2), kind=kCustom, calls=%fused_computation.1.clone.clone.1 | custom fusion | flops 1048576 | bytes 12583168 | tf_op jit(solution)/shard_map/while/body/scatter-add | solution.py:46
  706.8 151.4 %reduce-scatter.2.cloned.1.call-done = f32[2048,128]{1,0:T(8,128)} async-done(((f32[32768,128]{1,0:T(8,128)}), f32[2048,128]{1,0:T(8,128)}) %reduce-scatter.2.cloned.1.call-update) | async-done | bytes 1048592 | tf_op jit(solution)/shard_map/reduce_scatter | solution.py:63
  (196 shorter events, 282.7 us)
Async XLA Ops:
  6.5 1.0 copy-start
  6.5 107.8 %all-gather.2.cloned.1.call-start = ((), (), s32[]{:S(2)}) async-start(), calls=%async_computation.1 | async-start | bytes 8912896 | tf_op jit(solution)/shard_map/all_gather | solution.py:55
  9.4 848.8 %reduce-scatter.2.cloned.1.call-start = ((), (), s32[]{:S(2)}) async-start(), calls=%async_computation.2 | async-start | bytes 17825792 | tf_op jit(solution)/shard_map/reduce_scatter | solution.py:63
Sparse Core Ops, SparseCore 0:
  9.6 104.7 all-gather.1
  706.9 151.2 reduce-scatter.1
where the time goes:
time: 873 us; the launch traced here: 867 us
  local copies, waits for them, and re-layouts  289 us (33%)
  waiting for transfers between devices  256 us (29%)
  other arithmetic  235 us (27%)
  matrix products  72.5 us (8%)
  between operations  14.1 us (2%)
    gather x16, local copies, waits for them, and re-layouts, one_block(): gathered = column_block[sources].reshape(block, erows.shape[1], width)  248 us
    scatter-add x16, other arithmetic, one_block(): return accum.at[target].add(product)  209 us
    reduce_scatter x1, waiting for transfers between devices, local(): lax.psum_scatter(accum.reshape(block_rows, width), 'col', scatter_dimensi...  151 us
    all_gather x1, waiting for transfers between devices, local(): column_block = lax.all_gather(transformed, 'row', axis=0, tiled=True)  104 us
    dot_general x16, matrix products, one_block(): jnp.einsum('bte,bef->btf', row_table, gathered, preferred_element_type=jn...  70.7 us
    select_n x16, other arithmetic, one_block(): return accum.at[target].add(product)  22.8 us
  transfers between devices with their start and end apart: 2, of which 2 were waited for; matrix products, arithmetic and copies ran while one was open for 0% of the time, Pallas kernels for 0%

commit v1 on v0

v1 whole, which is shorter than its diff:
```python
import jax
import jax.numpy as jnp
from jax import lax
from jax.experimental import pallas as pl
from jax.experimental.pallas import tpu as pltpu
from jax.sharding import PartitionSpec as P

MESH = pl.DeviceIdType.MESH
BF, F32 = jnp.bfloat16, jnp.float32

TILE = 128
FEAT = 128
NODE = 2048
SLOTS = 1024
HALF = SLOTS // 2
EDGES = 64
ZN, YN = 8, 4
NT = NODE // TILE
EARLY = 7
LATE = NT - EARLY
HALVES = {1: (EARLY, LATE // 2), -1: (EARLY + LATE // 2, LATE - LATE // 2)}
PIECES = 4
PROWS = NODE // PIECES
X_FIRST = (False, True, False, True)
MIB = 2**20


def place():
    row, col = lax.axis_index("row"), lax.axis_index("col")
    return row // ZN, row % ZN, col // 4, (col // 2) % 2, col % 2


def device(xlo, z, y, xhi, core):
    return (xlo * ZN + z, y * 4 + xhi * 2 + core)


def add_rows(dst, dst_row, parts, rows, finish=None):
    step = 128

    def body(i, carry):
        total = None
        for ref, first in parts:
            term = ref[pl.ds(pl.multiple_of(first + i * step, 64), step), :].astype(F32)
            total = term if total is None else total + term
        if finish is not None:
            total = finish(total)
        dst[pl.ds(pl.multiple_of(dst_row + i * step, 64), step), :] = total.astype(BF)
        return carry

    lax.fori_loop(0, rows // step, body, 0, unroll=2)


def layer_kernel(
    tile_row, tile_col, ends,
    feat, weight, edge_row, edge_col, edge_weight,
    out,
    x, tiles, er2, ec2, ew2, acc, give, mine, got,
    y_in, yx_in, xy_in, x_in,
    send, recv,
):
    xlo, z, y, xhi, core = place()
    z_next = {1: device(xlo, (z + 1) % ZN, y, xhi, core), -1: device(xlo, (z + ZN - 1) % ZN, y, xhi, core)}
    y_next = {1: device(xlo, z, (y + 1) % YN, xhi, core), -1: device(xlo, z, (y + YN - 1) % YN, xhi, core)}
    x_pair = device(1 - xlo, z, y, xhi, core)
    x_far = device(xlo, z, y, 1 - xhi, core)
    sibling = device(xlo, z, y, xhi, 1 - core)

    barrier = pltpu.get_barrier_semaphore()
    others = [z_next[1], z_next[-1], y_next[1], y_next[-1], x_pair, x_far, sibling]
    for other in others:
        pl.semaphore_signal(barrier, inc=1, device_id=other, device_id_type=MESH)

    copies = []

    def start(src, dst, target):
        number = len(copies)
        copy = pltpu.make_async_remote_copy(
            src_ref=src, dst_ref=dst, send_sem=send.at[number], recv_sem=recv.at[number],
            device_id=target, device_id_type=MESH,
        )
        copy.start()
        copies.append(copy)
        return copy

    def block(i, zz):
        return (i * ZN + zz) * NT

    own = block(xlo, z)

    def transform(i, carry):
        rows = pl.ds(pl.multiple_of(i * 256, 256), 256)
        part = jnp.dot(feat[rows, :], weight[...], preferred_element_type=F32).astype(BF)
        x[pl.ds(own + i * 2, 2)] = part.reshape(2, TILE, FEAT)
        return carry

    lax.fori_loop(0, NODE // 256, transform, 0)

    lane = lax.broadcasted_iota(jnp.int32, (16, 128), 1)
    shift = jnp.where(lane >= EDGES, 128.0, 0.0)

    def prep(i, carry):
        first = pl.multiple_of(i * 16, 16)
        rows, later = pl.ds(first, 16), pl.ds(pl.multiple_of(first + HALF, 16), 16)

        def both(ref):
            return jnp.concatenate([ref[rows, :], ref[later, :]], axis=1).astype(F32)

        er2[rows, :] = both(edge_row)
        ec2[rows, :] = both(edge_col) + shift
        ew = jnp.concatenate([edge_weight[rows, :].astype(F32), edge_weight[later, :].astype(F32)], axis=1)
        ew2[rows, :] = ew
        return carry

    iota = lax.broadcasted_iota(jnp.int32, (256, 128), 0).astype(F32).astype(BF)
    GROUP = 4

    def build(i, carry):
        for u in range(GROUP):
            p = i * GROUP + u

            def spread(ref, n):
                return jnp.concatenate([jnp.broadcast_to(ref[pl.ds(p, 1), :], (16, 128)).astype(BF)] * n, axis=0)

            picks = jnp.where(spread(er2, 8) == iota[:128], spread(ew2, 8), jnp.zeros((128, 128), BF))
            sources = jnp.where(spread(ec2, 16) == iota, jnp.ones((256, 128), BF), jnp.zeros((256, 128), BF))
            dense = lax.dot_general(picks, sources, (((1,), (1,)), ((), ())), preferred_element_type=F32).astype(BF)
            tiles[p] = dense[:, :128]
            tiles[p + HALF] = dense[:, 128:]
        return carry

    built = [0]

    def build_some(n):
        first = built[0]
        lax.fori_loop(first, first + n, build, 0)
        built[0] = first + n

    def rows_of(i, zz, offset, n):
        return x.at[pl.ds(block(i, zz) + offset, n)]

    def ring(direction, hop, i, offset, n):
        ref = rows_of(i, (z - direction * (hop - 1) + ZN) % ZN, offset, n)
        return start(ref, ref, z_next[direction])

    def cross(direction, hop, offset, n):
        ref = rows_of(xlo, (z - direction * hop + ZN) % ZN, offset, n)
        return start(ref, ref, x_pair)

    late, early, pair_early = (xlo, EARLY, LATE), (xlo, 0, EARLY), (1 - xlo, 0, EARLY)
    pl.semaphore_wait(barrier, len(others))
    hops = {}
    for d in (1, -1):
        hops[1, d, "late"] = ring(d, 1, *late)
    cross_early = cross(1, 0, 0, EARLY)
    for d in (1, -1):
        hops[1, d, "early"] = ring(d, 1, *early)
    crossed = [cross(1, 0, EARLY, LATE)]
    lax.fori_loop(0, HALF // 16, prep, 0)
    build_some(8)
    cross_early.wait_recv()
    for d in (1, -1):
        hops[1, d, "pair"] = ring(d, 1, *pair_early)
    final = []
    for hop in (1, 2, 3):
        for name, part in (("late", late), ("early", early), ("pair", pair_early)):
            build_some(12)
            for d in (1, -1):
                hops[hop, d, name].wait_recv()
                if hop < 3:
                    hops[hop + 1, d, name] = ring(d, hop + 1, *part)
                elif name == "late":
                    hops[4, d, name] = ring(d, 4, xlo, *HALVES[d])
                elif (name == "early") == (d == 1):
                    final.append(ring(d, 4, *part))
                if name == "late":
                    crossed.append(cross(d, hop, EARLY, LATE))
    build_some(HALF // GROUP - built[0])
    for d in (1, -1):
        hops[4, d, "late"].wait_recv()
        crossed.append(cross(d, 4, *HALVES[d]))
    for copy in final + crossed:
        copy.wait_recv()

    acc[...] = jnp.zeros_like(acc)
    STEP = 8

    def accumulate(i, carry):
        products = []
        for u in range(STEP):
            s = i * STEP + u
            products.append(jnp.dot(tiles[s], x[tile_col[s]], preferred_element_type=F32))
        total = acc[...]
        for u in range(STEP):
            s = i * STEP + u
            step = tile_row[s] - tile_row[jnp.maximum(s - 1, 0)]
            keep = jnp.maximum(1 - jnp.maximum(step, 0), 0).astype(F32)
            total = total * keep + products[u]
            tiles[s] = total.astype(BF)
        acc[...] = total
        return carry

    lax.fori_loop(0, SLOTS // STEP, accumulate, 0)

    def emit(buffer, owner_core, j):
        def body(q, carry):
            xx, yy = q // YN, q % YN
            first = (yy * 4 + xx * 2 + owner_core) * (NODE // TILE) + j * (PROWS // TILE)
            for g in range(PROWS // TILE):
                end = ends[first + g + 1]
                found = jnp.minimum(end - ends[first + g], 1).astype(F32)
                total = tiles[jnp.maximum(end - 1, 0)] * jnp.full((TILE, FEAT), found, F32).astype(BF)
                buffer[j, pl.ds(pl.multiple_of(q * PROWS + g * TILE, TILE), TILE), :] = total
            return carry

        lax.fori_loop(0, 2 * YN, body, 0)

    given = []
    for j in range(PIECES):
        emit(give, 1 - core, j)
        given.append(start(give.at[j], got.at[j], sibling))
    for j in range(PIECES):
        emit(mine, core, j)

    def chunk(xx, yy):
        return (xx * YN + yy) * PROWS

    def at(ref, first, n):
        return ref.at[pl.ds(pl.multiple_of(first, 64), n)]

    up, down, far = (y + 1) % YN, (y + YN - 1) % YN, (y + 2) % YN
    h = PROWS // 2
    state = [None] * PIECES
    slot = {j: n for kind in (False, True) for n, j in enumerate([k for k in range(PIECES) if X_FIRST[k] == kind])}
    for j in range(PIECES):
        given[j].wait_recv()
        sums, land = mine.at[j], slot[j]
        add_rows(sums, 0, [(sums, 0), (got.at[j], 0)], 2 * YN * PROWS)
        if X_FIRST[j]:
            state[j] = start(at(sums, chunk(1 - xhi, 0), YN * PROWS), x_in.at[land], x_far)
        else:
            into = y_in.at[land]
            state[j] = [
                start(at(sums, chunk(0, far), PROWS), at(into, 0, PROWS), y_next[1]),
                start(at(sums, chunk(1, far), PROWS), at(into, PROWS, PROWS), y_next[-1]),
                start(at(sums, chunk(1, up), PROWS), at(into, 2 * PROWS, PROWS), y_next[1]),
                start(at(sums, chunk(0, down), PROWS), at(into, 3 * PROWS, PROWS), y_next[-1]),
            ]
    for j in range(PIECES):
        sums, land = mine.at[j], slot[j]
        if X_FIRST[j]:
            state[j].wait_recv()
            into, base = xy_in.at[land], chunk(xhi, 0)
            add_rows(sums, base, [(sums, base), (x_in.at[land], 0)], YN * PROWS)
            state[j] = [
                start(at(sums, chunk(xhi, far), h), at(into, 0, h), y_next[1]),
                start(at(sums, chunk(xhi, far) + h, h), at(into, h, h), y_next[-1]),
                start(at(sums, chunk(xhi, up) + h, h), at(into, 2 * h, h), y_next[1]),
                start(at(sums, chunk(xhi, down), h), at(into, 3 * h, h), y_next[-1]),
            ]
        else:
            into = y_in.at[land]
            state[j][0].wait_recv()
            add_rows(sums, chunk(0, up), [(sums, chunk(0, up)), (into, 0)], PROWS)
            state[j].append(start(at(sums, chunk(0, up), PROWS), at(into, 4 * PROWS, PROWS), y_next[1]))
            state[j][1].wait_recv()
            add_rows(sums, chunk(1, down), [(sums, chunk(1, down)), (into, PROWS)], PROWS)
            state[j].append(start(at(sums, chunk(1, down), PROWS), at(into, 5 * PROWS, PROWS), y_next[-1]))
    for j in range(PIECES):
        sums, land = mine.at[j], slot[j]
        if X_FIRST[j]:
            into = xy_in.at[land]
            state[j][0].wait_recv()
            add_rows(sums, chunk(xhi, up), [(sums, chunk(xhi, up)), (into, 0)], h)
            state[j].append(start(at(sums, chunk(xhi, up), h), at(into, 4 * h, h), y_next[1]))
            state[j][1].wait_recv()
            add_rows(sums, chunk(xhi, down) + h, [(sums, chunk(xhi, down) + h), (into, h)], h)
            state[j].append(start(at(sums, chunk(xhi, down) + h, h), at(into, 5 * h, h), y_next[-1]))
        else:
            into = y_in.at[land]
            for copy in state[j][2:]:
                copy.wait_recv()
            low = (4, 3)
            high = (2, 5)
            for xx, (one, two) in ((0, low), (1, high)):
                add_rows(
                    sums, chunk(xx, y), [(sums, chunk(xx, y)), (into, one * PROWS), (into, two * PROWS)], PROWS
                )
            state[j] = start(at(sums, chunk(1 - xhi, y), PROWS), yx_in.at[land], x_far)
    relu = lambda v: jnp.maximum(v, 0.0)
    for j in range(PIECES):
        sums, land = mine.at[j], slot[j]
        if X_FIRST[j]:
            into, base = xy_in.at[land], chunk(xhi, y)
            for copy in state[j][2:]:
                copy.wait_recv()
            add_rows(out, j * PROWS, [(sums, base), (into, 4 * h), (into, 3 * h)], h, relu)
            add_rows(out, j * PROWS + h, [(sums, base + h), (into, 2 * h), (into, 5 * h)], h, relu)
        else:
            state[j].wait_recv()
            add_rows(out, j * PROWS, [(sums, chunk(xhi, y)), (yx_in.at[land], 0)], PROWS, relu)
    for copy in copies:
        copy.wait_send()


def local(features, weight, tile_row, tile_col, tile_count, edge_row, edge_col, edge_weight):
    live = jnp.arange(SLOTS, dtype=jnp.int32) < tile_count[0]
    starts = jnp.arange(257, dtype=jnp.int32)
    ends = jnp.sum(((tile_row[None, :] < starts[:, None]) & live[None, :]).astype(jnp.int32), axis=1)
    smem = pl.BlockSpec(memory_space=pltpu.SMEM)
    vmem = pl.BlockSpec(memory_space=pltpu.VMEM)
    n_y, n_x = X_FIRST.count(False), X_FIRST.count(True)
    copies = 64 + 8 * PIECES
    return pl.pallas_call(
        layer_kernel,
        out_shape=jax.ShapeDtypeStruct((NODE, FEAT), BF),
        in_specs=[smem] * 3 + [vmem] * 5,
        out_specs=vmem,
        scratch_shapes=[
            pltpu.VMEM((16 * NT, TILE, FEAT), BF),
            pltpu.VMEM((SLOTS, TILE, FEAT), BF),
            pltpu.VMEM((HALF, 128), F32),
            pltpu.VMEM((HALF, 128), F32),
            pltpu.VMEM((HALF, 128), F32),
            pltpu.VMEM((TILE, FEAT), F32),
            pltpu.VMEM((PIECES, 2 * YN * PROWS, FEAT), BF),
            pltpu.VMEM((PIECES, 2 * YN * PROWS, FEAT), BF),
            pltpu.VMEM((PIECES, 2 * YN * PROWS, FEAT), BF),
            pltpu.VMEM((n_y, 6 * PROWS, FEAT), BF),
            pltpu.VMEM((n_y, PROWS, FEAT), BF),
            pltpu.VMEM((n_x, 3 * PROWS, FEAT), BF),
            pltpu.VMEM((n_x, YN * PROWS, FEAT), BF),
            pltpu.SemaphoreType.DMA((copies,)),
            pltpu.SemaphoreType.DMA((copies,)),
        ],
        compiler_params=pltpu.CompilerParams(
            collective_id=0, has_side_effects=True, vmem_limit_bytes=62 * MIB
        ),
        cost_estimate=pl.CostEstimate(flops=9 * 10**9, bytes_accessed=4 * MIB, transcendentals=0),
        name="graph_layer",
    )(tile_row, tile_col, ends, features, weight, edge_row, edge_col, edge_weight)


def solution(mesh):
    in_specs = (
        P(("col", "row"), None),
        P(),
        P(("row", "col")),
        P(("row", "col")),
        P(("row", "col")),
        P(("row", "col"), None),
        P(("row", "col"), None),
        P(("row", "col"), None),
    )
    out_specs = P(("row", "col"), None)
    return jax.shard_map(local, mesh=mesh, in_specs=in_specs, out_specs=out_specs, check_vma=False)
```

time: 873 us -> 148 us (0.17)
  local copies, waits for them, and re-layouts: 289 us -> 5.67 us
  waiting for transfers between devices: 256 us -> 0 us
  other arithmetic: 235 us -> 1.5 us
  Pallas kernels: 0 us -> 140 us
  matrix products: 72.5 us -> 0 us
  between operations: 14.1 us -> 0.71 us
    gather x16 -> x0, local copies, waits for them, and re-layouts: 248 us -> none  [one_block(): gathered = column_block[sources].reshape(block, erows.shape[1], width)]
    scatter-add x16 -> x0, other arithmetic: 209 us -> none  [one_block(): return accum.at[target].add(product)]
    reduce_scatter x1 -> x0, waiting for transfers between devices: 151 us -> none  [local(): lax.psum_scatter(accum.reshape(block_rows, width), 'col', scatter_dimensi...]
    pallas_call x0 -> x1, Pallas kernels: none -> 140 us  [local(): pl.pallas_call(layer_kernel, out_shape=jax.ShapeDtypeStruct((NODE, FEAT),...]
    all_gather x1 -> x0, waiting for transfers between devices: 104 us -> none  [local(): column_block = lax.all_gather(transformed, 'row', axis=0, tiled=True)]
    dot_general x17 -> x0, matrix products: 72.5 us -> none  [the longest x16 70.7 us: one_block(): jnp.einsum('bte,bef->btf', row_table, gathered, preferred_element_type=jn...]
    dynamic_slice x80 -> x0, local copies, waits for them, and re-layouts: 30.4 us -> none  [the longest x32 15 us: one_block(): ecols = lax.dynamic_slice_in_dim(edge_col, begin, block, 0)]
    select_n x32 -> x0, other arithmetic: 23.1 us -> none  [the longest x16 22.8 us: one_block(): return accum.at[target].add(product)]
  transfers between devices with their start and end apart: 2 -> 0, of which waited for: 2 -> 0; matrix products, arithmetic and copies ran while one was open for 0% -> 0% of each run, Pallas kernels for 0% -> 0%
where the time goes in v1:
time: 148 us
  Pallas kernels  140 us (95%)
  local copies, waits for them, and re-layouts  5.67 us (4%)
  other arithmetic  1.5 us (1%)
    pallas_call x1, Pallas kernels, local(): pl.pallas_call(layer_kernel, out_shape=jax.ShapeDtypeStruct((NODE, FEAT),...  140 us
    unnamed x8, local copies, waits for them, and re-layouts  5.67 us

profile of v1, /device:TPU:1, one launch (start us, length us, event | category | flops | bytes accessed | tf_op | source)
XLA Modules:
  0.0 148.1 jit_solution(1925274467164329033)
XLA Ops:
  0.0 0.0 copy-start
  0.7 1.5 %convert_reduce_fusion.ends = s32[257]{0:T(512)} fusion(s32[1024]{0:T(1024)} %tile_row.1, pred[1024]{0:T(1024)(128)(4,1)S(1)} %iota_compare_fusion.1), kind=kLoop, calls=%fused_computation | loop fusion | flops 1052415 | bytes 6148 | tf_op jit(solution)/shard_map/reduce_sum | solution.py:308
  2.2 0.0 copy-start.1
  2.2 1.8 %copy.14.edge_weight = bf16[1024,64]{1,0:T(8,128)(2,1)} copy(bf16[1024,64]{0,1:T(8,128)(2,1)} %param.15) | data formatting | bytes 262144 | tf_op args[7]
  4.0 0.0 copy-done
  4.0 1.0 copy.12.edge_row
  5.0 0.0 copy-done.1
  5.0 1.0 copy.13.edge_col
  6.0 140.2 %graph_layer.1 = bf16[2048,128]{1,0:T(8,128)(2,1)} custom-call(s32[1024]{0:T(1024)} %tile_row.1, s32[1024]{0:T(1024)} %tile_col.1, s32[257]{0:T(512)} %convert_reduce_fusion.ends, bf16[2048,128]{1,0:T(8,128)(2,1)} %feat.1, bf16[128,128]{1,0:T(8,128)(2,1)} %weight.1, s32[1024,64]{1,0:T(8,128)} %copy.12.edge_row, s32[1024,64]{1,0:T(8,128)} %copy.13.edge_col, ...), custom_call_target="tpu_custom_call" | custom-call | flops 8999999488 | bytes 4194304 | tf_op jit(solution)/shard_map/graph_layer/pallas_call | solution.py:313
  146.3 1.9 %copy.17 = bf16[2048,128]{1,0:T(8,128)(2,1)} copy(bf16[2048,128]{1,0:T(8,128)(2,1)} %graph_layer.1) | data formatting | bytes 1048576
  (1 shorter events, 0.0 us)
Async XLA Ops:
  0.0 4.0 %copy-start = (s32[1024,64]{0,1:T(8,128)S(1)}, s32[1024,64]{0,1:T(8,128)}, u32[]{:S(2)}) copy-start(s32[1024,64]{0,1:T(8,128)} %param.13) | copy-start | bytes 786436
  2.2 2.8 %copy-start.1 = (s32[1024,64]{0,1:T(8,128)S(1)}, s32[1024,64]{0,1:T(8,128)}, u32[]{:S(2)}) copy-start(s32[1024,64]{0,1:T(8,128)} %param.14) | copy-start | bytes 786436

commit v2 on v1

--- a/solution.py
+++ b/solution.py
@@ -12,6 +12,7 @@
 FEAT = 128
 NODE = 2048
 SLOTS = 1024
+ENDS = 260
 HALF = SLOTS // 2
 EDGES = 64
 ZN, YN = 8, 4
@@ -19,9 +20,12 @@
 EARLY = 7
 LATE = NT - EARLY
 HALVES = {1: (EARLY, LATE // 2), -1: (EARLY + LATE // 2, LATE - LATE // 2)}
-PIECES = 4
+PIECES = 8
 PROWS = NODE // PIECES
-X_FIRST = (False, True, False, True)
+X_FIRST = (True, False, True, False, True, False, False, False)
+AHEAD = 2
+FIRSTS = (0, 1, 2, 3, 4, 5, 6, 7)
+LATER = (1, 3, 5, 6, 7, 0, 2, 4)
 MIB = 2**20
 
 
@@ -35,7 +39,7 @@
 
 
 def add_rows(dst, dst_row, parts, rows, finish=None):
-    step = 128
+    step = min(rows, 512)
 
     def body(i, carry):
         total = None
@@ -47,16 +51,16 @@
         dst[pl.ds(pl.multiple_of(dst_row + i * step, 64), step), :] = total.astype(BF)
         return carry
 
-    lax.fori_loop(0, rows // step, body, 0, unroll=2)
+    lax.fori_loop(0, rows // step, body, 0)
 
 
 def layer_kernel(
-    tile_row, tile_col, ends,
+    tile_row, tile_col, count_ref,
     feat, weight, edge_row, edge_col, edge_weight,
     out,
     x, tiles, er2, ec2, ew2, acc, give, mine, got,
     y_in, yx_in, xy_in, x_in,
-    send, recv,
+    ends, send, recv,
 ):
     xlo, z, y, xhi, core = place()
     z_next = {1: device(xlo, (z + 1) % ZN, y, xhi, core), -1: device(xlo, (z + ZN - 1) % ZN, y, xhi, core)}
@@ -95,20 +99,20 @@
 
     lax.fori_loop(0, NODE // 256, transform, 0)
 
-    lane = lax.broadcasted_iota(jnp.int32, (16, 128), 1)
-    shift = jnp.where(lane >= EDGES, 128.0, 0.0)
-
     def prep(i, carry):
-        first = pl.multiple_of(i * 16, 16)
-        rows, later = pl.ds(first, 16), pl.ds(pl.multiple_of(first + HALF, 16), 16)
+        rows = pl.ds(pl.multiple_of(i * 128, 128), 128)
 
         def both(ref):
-            return jnp.concatenate([ref[rows, :], ref[later, :]], axis=1).astype(F32)
-
-        er2[rows, :] = both(edge_row)
-        ec2[rows, :] = both(edge_col) + shift
-        ew = jnp.concatenate([edge_weight[rows, :].astype(F32), edge_weight[later, :].astype(F32)], axis=1)
-        ew2[rows, :] = ew
+            first = ref[:, pl.ds(pl.multiple_of(i * 128, 128), 128)].astype(F32)
+            later = ref[:, pl.ds(pl.multiple_of(i * 128 + HALF, 128), 128)].astype(F32)
+            return first, later
+
+        first, later = both(edge_row)
+        er2[rows, :] = jnp.concatenate([first, later], axis=0).T
+        first, later = both(edge_col)
+        ec2[rows, :] = jnp.concatenate([first, later + 128.0], axis=0).T
+        first, later = both(edge_weight)
+        ew2[rows, :] = jnp.concatenate([first, later], axis=0).T
         return carry
 
     iota = lax.broadcasted_iota(jnp.int32, (256, 128), 0).astype(F32).astype(BF)
@@ -127,6 +131,31 @@
             tiles[p] = dense[:, :128]
             tiles[p + HALF] = dense[:, 128:]
         return carry
+
+    count = count_ref[0]
+    ROWS_AT_ONCE = 4
+
+    def unit(v):
+        return jnp.minimum(jnp.maximum(v, 0), 1)
+
+    def bisect(i, carry):
+        rows = [i * ROWS_AT_ONCE + u for u in range(ROWS_AT_ONCE)]
+        found = [i * 0 for row in rows]
+        for step in (512, 256, 128, 64, 32, 16, 8, 4, 2, 1, 1):
+            for u, row in enumerate(rows):
+                probe = found[u] + step
+                below = unit(row - tile_row[jnp.minimum(probe, SLOTS) - 1])
+                found[u] = found[u] + step * below * unit(count + 1 - probe)
+        for u, row in enumerate(rows):
+            ends[row] = found[u]
+        return carry
+
+    bisected = [0]
+
+    def bisect_some(n):
+        first = bisected[0]
+        lax.fori_loop(first, min(first + n, ENDS // ROWS_AT_ONCE), bisect, 0)
+        bisected[0] = min(first + n, ENDS // ROWS_AT_ONCE)
 
     built = [0]
 
@@ -155,7 +184,7 @@
     for d in (1, -1):
         hops[1, d, "early"] = ring(d, 1, *early)
     crossed = [cross(1, 0, EARLY, LATE)]
-    lax.fori_loop(0, HALF // 16, prep, 0)
+    lax.fori_loop(0, HALF // 128, prep, 0)
     build_some(8)
     cross_early.wait_recv()
     for d in (1, -1):
@@ -164,6 +193,7 @@
     for hop in (1, 2, 3):
         for name, part in (("late", late), ("early", early), ("pair", pair_early)):
             build_some(12)
+            bisect_some(8)
             for d in (1, -1):
                 hops[hop, d, name].wait_recv()
                 if hop < 3:
@@ -182,7 +212,7 @@
         copy.wait_recv()
 
     acc[...] = jnp.zeros_like(acc)
-    STEP = 8
+    STEP = 64
 
     def accumulate(i, carry):
         products = []
@@ -201,7 +231,7 @@
 
     lax.fori_loop(0, SLOTS // STEP, accumulate, 0)
 
-    def emit(buffer, owner_core, j):
+    def emit(buffer, owner_core, j, received):
         def body(q, carry):
             xx, yy = q // YN, q % YN
             first = (yy * 4 + xx * 2 + owner_core) * (NODE // TILE) + j * (PROWS // TILE)
@@ -209,17 +239,19 @@
                 end = ends[first + g + 1]
                 found = jnp.minimum(end - ends[first + g], 1).astype(F32)
                 total = tiles[jnp.maximum(end - 1, 0)] * jnp.full((TILE, FEAT), found, F32).astype(BF)
-                buffer[j, pl.ds(pl.multiple_of(q * PROWS + g * TILE, TILE), TILE), :] = total
+                rows = pl.ds(pl.multiple_of(q * PROWS + g * TILE, TILE), TILE)
+                if received is not None:
+                    total = total + received[j, rows, :]
+                buffer[j, rows, :] = total
             return carry
 
-        lax.fori_loop(0, 2 * YN, body, 0)
+        lax.fori_loop(0, 2 * YN, body, 0, unroll=4)
 
     given = []
-    for j in range(PIECES):
-        emit(give, 1 - core, j)
+
+    def hand_over(j):
+        emit(give, 1 - core, j, None)
         given.append(start(give.at[j], got.at[j], sibling))
-    for j in range(PIECES):
-        emit(mine, core, j)
 
     def chunk(xx, yy):
         return (xx * YN + yy) * PROWS
@@ -231,10 +263,10 @@
     h = PROWS // 2
     state = [None] * PIECES
     slot = {j: n for kind in (False, True) for n, j in enumerate([k for k in range(PIECES) if X_FIRST[k] == kind])}
-    for j in range(PIECES):
+    def finish_a(j):
         given[j].wait_recv()
         sums, land = mine.at[j], slot[j]
-        add_rows(sums, 0, [(sums, 0), (got.at[j], 0)], 2 * YN * PROWS)
+        emit(mine, core, j, got)
         if X_FIRST[j]:
             state[j] = start(at(sums, chunk(1 - xhi, 0), YN * PROWS), x_in.at[land], x_far)
         else:
@@ -245,7 +277,8 @@
                 start(at(sums, chunk(1, up), PROWS), at(into, 2 * PROWS, PROWS), y_next[1]),
                 start(at(sums, chunk(0, down), PROWS), at(into, 3 * PROWS, PROWS), y_next[-1]),
             ]
-    for j in range(PIECES):
+
+    def stage_b(j):
         sums, land = mine.at[j], slot[j]
         if X_FIRST[j]:
             state[j].wait_recv()
@@ -265,7 +298,8 @@
             state[j][1].wait_recv()
             add_rows(sums, chunk(1, down), [(sums, chunk(1, down)), (into, PROWS)], PROWS)
             state[j].append(start(at(sums, chunk(1, down), PROWS), at(into, 5 * PROWS, PROWS), y_next[-1]))
-    for j in range(PIECES):
+
+    def stage_c(j):
         sums, land = mine.at[j], slot[j]
         if X_FIRST[j]:
             into = xy_in.at[land]
@@ -286,8 +320,8 @@
                     sums, chunk(xx, y), [(sums, chunk(xx, y)), (into, one * PROWS), (into, two * PROWS)], PROWS
                 )
             state[j] = start(at(sums, chunk(1 - xhi, y), PROWS), yx_in.at[land], x_far)
-    relu = lambda v: jnp.maximum(v, 0.0)
-    for j in range(PIECES):
+
+    def stage_d(j):
         sums, land = mine.at[j], slot[j]
         if X_FIRST[j]:
             into, base = xy_in.at[land], chunk(xhi, y)
@@ -298,14 +332,22 @@
         else:
             state[j].wait_recv()
             add_rows(out, j * PROWS, [(sums, chunk(xhi, y)), (yx_in.at[land], 0)], PROWS, relu)
+
+    relu = lambda v: jnp.maximum(v, 0.0)
+    stages = {"a": finish_a, "b": stage_b, "c": stage_c, "d": stage_d}
+    steps = [("a", j) for j in FIRSTS] + [(stage, j) for stage in "bcd" for j in LATER]
+    handed = 0
+    for stage, j in steps:
+        if stage == "a":
+            while handed < min(FIRSTS.index(j) + 1 + AHEAD, PIECES):
+                hand_over(FIRSTS[handed])
+                handed += 1
+        stages[stage](j)
     for copy in copies:
         copy.wait_send()
 
 
 def local(features, weight, tile_row, tile_col, tile_count, edge_row, edge_col, edge_weight):
-    live = jnp.arange(SLOTS, dtype=jnp.int32) < tile_count[0]
-    starts = jnp.arange(257, dtype=jnp.int32)
-    ends = jnp.sum(((tile_row[None, :] < starts[:, None]) & live[None, :]).astype(jnp.int32), axis=1)
     smem = pl.BlockSpec(memory_space=pltpu.SMEM)
     vmem = pl.BlockSpec(memory_space=pltpu.VMEM)
     n_y, n_x = X_FIRST.count(False), X_FIRST.count(True)
@@ -329,6 +371,7 @@
             pltpu.VMEM((n_y, PROWS, FEAT), BF),
             pltpu.VMEM((n_x, 3 * PROWS, FEAT), BF),
             pltpu.VMEM((n_x, YN * PROWS, FEAT), BF),
+            pltpu.SMEM((ENDS,), jnp.int32),
             pltpu.SemaphoreType.DMA((copies,)),
             pltpu.SemaphoreType.DMA((copies,)),
         ],
@@ -337,7 +380,7 @@
         ),
         cost_estimate=pl.CostEstimate(flops=9 * 10**9, bytes_accessed=4 * MIB, transcendentals=0),
         name="graph_layer",
-    )(tile_row, tile_col, ends, features, weight, edge_row, edge_col, edge_weight)
+    )(tile_row, tile_col, tile_count, features, weight, edge_row.T, edge_col.T, edge_weight.T)
 
 
 def solution(mesh):

time: 148 us -> 120 us (0.81)
  Pallas kernels: 140 us -> 117 us
  local copies, waits for them, and re-layouts: 5.67 us -> 1.87 us
  other arithmetic: 1.5 us -> 0 us
    pallas_call x1, Pallas kernels: 140 us -> 117 us  [local(): pl.pallas_call(layer_kernel, out_shape=jax.ShapeDtypeStruct((NODE, FEAT),...]
    unnamed x8 -> x1, local copies, waits for them, and re-layouts: 5.67 us -> 1.87 us
    reduce_sum x1 -> x0, other arithmetic: 1.5 us -> none  [local(): jnp.sum(((tile_row[None, :] < starts[:, None]) & live[None, :]).astype(jn...]
where the time goes in v2:
time: 120 us
  Pallas kernels  117 us (98%)
  local copies, waits for them, and re-layouts  1.87 us (2%)
    pallas_call x1, Pallas kernels, local(): pl.pallas_call(layer_kernel, out_shape=jax.ShapeDtypeStruct((NODE, FEAT),...  117 us

profile of v2, /device:TPU:1, one launch (start us, length us, event | category | flops | bytes accessed | tf_op | source)
XLA Modules:
  0.0 119.7 jit_solution(15098793825421195808)
XLA Ops:
  0.7 117.1 %graph_layer.1 = bf16[2048,128]{1,0:T(8,128)(2,1)} custom-call(s32[1024]{0:T(1024)} %tile_row.1, s32[1024]{0:T(1024)} %tile_col.1, s32[1]{0:T(128)S(6)} %copy.10.count_ref, bf16[2048,128]{1,0:T(8,128)(2,1)} %feat.1, bf16[128,128]{1,0:T(8,128)(2,1)} %weight.1, s32[64,1024]{1,0:T(8,128)} %bitcast.3, s32[64,1024]{1,0:T(8,128)} %bitcast.4, bf16[64,1024]{1,0:T(8,128)(2,1)} %bitcast.5), custom_call_target="tpu_custom_call" | custom-call | flops 8999999488 | bytes 4194304 | tf_op jit(solution)/shard_map/graph_layer/pallas_call | solution.py:355
  117.8 1.9 %copy.11 = bf16[2048,128]{1,0:T(8,128)(2,1)} copy(bf16[2048,128]{1,0:T(8,128)(2,1)} %graph_layer.1) | data formatting | bytes 1048576

commit v3 on v2

--- a/solution.py
+++ b/solution.py
@@ -21,7 +21,8 @@
 LATE = NT - EARLY
 HALVES = {1: (EARLY, LATE // 2), -1: (EARLY + LATE // 2, LATE - LATE // 2)}
 PIECES = 8
-PROWS = NODE // PIECES
+PT = NT // PIECES
+CHUNKS = 2 * YN * PT
 X_FIRST = (True, False, True, False, True, False, False, False)
 AHEAD = 2
 FIRSTS = (0, 1, 2, 3, 4, 5, 6, 7)
@@ -38,27 +39,27 @@
     return (xlo * ZN + z, y * 4 + xhi * 2 + core)
 
 
-def add_rows(dst, dst_row, parts, rows, finish=None):
-    step = min(rows, 512)
+def add_tiles(dst, dst_tile, parts, tiles, finish=None):
+    step = min(tiles, 4)
 
     def body(i, carry):
         total = None
         for ref, first in parts:
-            term = ref[pl.ds(pl.multiple_of(first + i * step, 64), step), :].astype(F32)
+            term = ref[pl.ds(first + i * step, step)].astype(F32)
             total = term if total is None else total + term
         if finish is not None:
             total = finish(total)
-        dst[pl.ds(pl.multiple_of(dst_row + i * step, 64), step), :] = total.astype(BF)
-        return carry
-
-    lax.fori_loop(0, rows // step, body, 0)
+        dst[pl.ds(dst_tile + i * step, step)] = total.astype(BF)
+        return carry
+
+    lax.fori_loop(0, tiles // step, body, 0)
 
 
 def layer_kernel(
     tile_row, tile_col, count_ref,
     feat, weight, edge_row, edge_col, edge_weight,
     out,
-    x, tiles, er2, ec2, ew2, acc, give, mine, got,
+    x, tiles, er2, ec2, ew2, acc, got,
     y_in, yx_in, xy_in, x_in,
     ends, send, recv,
 ):
@@ -212,7 +213,7 @@
         copy.wait_recv()
 
     acc[...] = jnp.zeros_like(acc)
-    STEP = 64
+    STEP = 128
 
     def accumulate(i, carry):
         products = []
@@ -231,59 +232,64 @@
 
     lax.fori_loop(0, SLOTS // STEP, accumulate, 0)
 
+    for copy in copies:
+        copy.wait_send()
+    gathered = len(copies)
+    give = [x.at[pl.ds(j * CHUNKS, CHUNKS)] for j in range(PIECES)]
+    mine = [x.at[pl.ds((PIECES + j) * CHUNKS, CHUNKS)] for j in range(PIECES)]
+
     def emit(buffer, owner_core, j, received):
         def body(q, carry):
             xx, yy = q // YN, q % YN
-            first = (yy * 4 + xx * 2 + owner_core) * (NODE // TILE) + j * (PROWS // TILE)
-            for g in range(PROWS // TILE):
+            first = (yy * 4 + xx * 2 + owner_core) * NT + j * PT
+            for g in range(PT):
                 end = ends[first + g + 1]
                 found = jnp.minimum(end - ends[first + g], 1).astype(F32)
                 total = tiles[jnp.maximum(end - 1, 0)] * jnp.full((TILE, FEAT), found, F32).astype(BF)
-                rows = pl.ds(pl.multiple_of(q * PROWS + g * TILE, TILE), TILE)
                 if received is not None:
-                    total = total + received[j, rows, :]
-                buffer[j, rows, :] = total
+                    total = total + received[q * PT + g]
+                buffer[q * PT + g] = total
             return carry
 
         lax.fori_loop(0, 2 * YN, body, 0, unroll=4)
 
-    given = []
+    given = {}
 
     def hand_over(j):
-        emit(give, 1 - core, j, None)
-        given.append(start(give.at[j], got.at[j], sibling))
+        emit(give[j], 1 - core, j, None)
+        given[j] = start(give[j], got.at[j], sibling)
 
     def chunk(xx, yy):
-        return (xx * YN + yy) * PROWS
+        return (xx * YN + yy) * PT
 
     def at(ref, first, n):
-        return ref.at[pl.ds(pl.multiple_of(first, 64), n)]
+        return ref.at[pl.ds(first, n)]
 
     up, down, far = (y + 1) % YN, (y + YN - 1) % YN, (y + 2) % YN
-    h = PROWS // 2
+    h = PT // 2
     state = [None] * PIECES
     slot = {j: n for kind in (False, True) for n, j in enumerate([k for k in range(PIECES) if X_FIRST[k] == kind])}
     def finish_a(j):
         given[j].wait_recv()
-        sums, land = mine.at[j], slot[j]
-        emit(mine, core, j, got)
+        sums, land = mine[j], slot[j]
+        emit(mine[j], core, j, got.at[j])
         if X_FIRST[j]:
-            state[j] = start(at(sums, chunk(1 - xhi, 0), YN * PROWS), x_in.at[land], x_far)
+            state[j] = start(at(sums, chunk(1 - xhi, 0), YN * PT), x_in.at[land], x_far)
         else:
             into = y_in.at[land]
             state[j] = [
-                start(at(sums, chunk(0, far), PROWS), at(into, 0, PROWS), y_next[1]),
-                start(at(sums, chunk(1, far), PROWS), at(into, PROWS, PROWS), y_next[-1]),
-                start(at(sums, chunk(1, up), PROWS), at(into, 2 * PROWS, PROWS), y_next[1]),
-                start(at(sums, chunk(0, down), PROWS), at(into, 3 * PROWS, PROWS), y_next[-1]),
+                start(at(sums, chunk(0, far), PT), at(into, 0, PT), y_next[1]),
+                start(at(sums, chunk(1, far), PT), at(into, PT, PT), y_next[-1]),
+                start(at(sums, chunk(1, up), PT), at(into, 2 * PT, PT), y_next[1]),
+                start(at(sums, chunk(0, down), PT), at(into, 3 * PT, PT), y_next[-1]),
             ]
 
     def stage_b(j):
-        sums, land = mine.at[j], slot[j]
+        sums, land = mine[j], slot[j]
         if X_FIRST[j]:
             state[j].wait_recv()
             into, base = xy_in.at[land], chunk(xhi, 0)
-            add_rows(sums, base, [(sums, base), (x_in.at[land], 0)], YN * PROWS)
+            add_tiles(sums, base, [(sums, base), (x_in.at[land], 0)], YN * PT)
             state[j] = [
                 start(at(sums, chunk(xhi, far), h), at(into, 0, h), y_next[1]),
                 start(at(sums, chunk(xhi, far) + h, h), at(into, h, h), y_next[-1]),
@@ -293,21 +299,21 @@
         else:
             into = y_in.at[land]
             state[j][0].wait_recv()
-            add_rows(sums, chunk(0, up), [(sums, chunk(0, up)), (into, 0)], PROWS)
-            state[j].append(start(at(sums, chunk(0, up), PROWS), at(into, 4 * PROWS, PROWS), y_next[1]))
+            add_tiles(sums, chunk(0, up), [(sums, chunk(0, up)), (into, 0)], PT)
+            state[j].append(start(at(sums, chunk(0, up), PT), at(into, 4 * PT, PT), y_next[1]))
             state[j][1].wait_recv()
-            add_rows(sums, chunk(1, down), [(sums, chunk(1, down)), (into, PROWS)], PROWS)
-            state[j].append(start(at(sums, chunk(1, down), PROWS), at(into, 5 * PROWS, PROWS), y_next[-1]))
+            add_tiles(sums, chunk(1, down), [(sums, chunk(1, down)), (into, PT)], PT)
+            state[j].append(start(at(sums, chunk(1, down), PT), at(into, 5 * PT, PT), y_next[-1]))
 
     def stage_c(j):
-        sums, land = mine.at[j], slot[j]
+        sums, land = mine[j], slot[j]
         if X_FIRST[j]:
             into = xy_in.at[land]
             state[j][0].wait_recv()
-            add_rows(sums, chunk(xhi, up), [(sums, chunk(xhi, up)), (into, 0)], h)
+            add_tiles(sums, chunk(xhi, up), [(sums, chunk(xhi, up)), (into, 0)], h)
             state[j].append(start(at(sums, chunk(xhi, up), h), at(into, 4 * h, h), y_next[1]))
             state[j][1].wait_recv()
-            add_rows(sums, chunk(xhi, down) + h, [(sums, chunk(xhi, down) + h), (into, h)], h)
+            add_tiles(sums, chunk(xhi, down) + h, [(sums, chunk(xhi, down) + h), (into, h)], h)
             state[j].append(start(at(sums, chunk(xhi, down) + h, h), at(into, 5 * h, h), y_next[-1]))
         else:
             into = y_in.at[land]
@@ -316,22 +322,22 @@
             low = (4, 3)
             high = (2, 5)
             for xx, (one, two) in ((0, low), (1, high)):
-                add_rows(
-                    sums, chunk(xx, y), [(sums, chunk(xx, y)), (into, one * PROWS), (into, two * PROWS)], PROWS
+                add_tiles(
+                    sums, chunk(xx, y), [(sums, chunk(xx, y)), (into, one * PT), (into, two * PT)], PT
                 )
-            state[j] = start(at(sums, chunk(1 - xhi, y), PROWS), yx_in.at[land], x_far)
+            state[j] = start(at(sums, chunk(1 - xhi, y), PT), yx_in.at[land], x_far)
 
     def stage_d(j):
-        sums, land = mine.at[j], slot[j]
+        sums, land = mine[j], slot[j]
         if X_FIRST[j]:
             into, base = xy_in.at[land], chunk(xhi, y)
             for copy in state[j][2:]:
                 copy.wait_recv()
-            add_rows(out, j * PROWS, [(sums, base), (into, 4 * h), (into, 3 * h)], h, relu)
-            add_rows(out, j * PROWS + h, [(sums, base + h), (into, 2 * h), (into, 5 * h)], h, relu)
+            add_tiles(out, j * PT, [(sums, base), (into, 4 * h), (into, 3 * h)], h, relu)
+            add_tiles(out, j * PT + h, [(sums, base + h), (into, 2 * h), (into, 5 * h)], h, relu)
         else:
             state[j].wait_recv()
-            add_rows(out, j * PROWS, [(sums, chunk(xhi, y)), (yx_in.at[land], 0)], PROWS, relu)
+            add_tiles(out, j * PT, [(sums, chunk(xhi, y)), (yx_in.at[land], 0)], PT, relu)
 
     relu = lambda v: jnp.maximum(v, 0.0)
     stages = {"a": finish_a, "b": stage_b, "c": stage_c, "d": stage_d}
@@ -343,7 +349,7 @@
                 hand_over(FIRSTS[handed])
                 handed += 1
         stages[stage](j)
-    for copy in copies:
+    for copy in copies[gathered:]:
         copy.wait_send()
 
 
@@ -354,7 +360,7 @@
     copies = 64 + 8 * PIECES
     return pl.pallas_call(
         layer_kernel,
-        out_shape=jax.ShapeDtypeStruct((NODE, FEAT), BF),
+        out_shape=jax.ShapeDtypeStruct((NT, TILE, FEAT), BF),
         in_specs=[smem] * 3 + [vmem] * 5,
         out_specs=vmem,
         scratch_shapes=[
@@ -364,13 +370,11 @@
             pltpu.VMEM((HALF, 128), F32),
             pltpu.VMEM((HALF, 128), F32),
             pltpu.VMEM((TILE, FEAT), F32),
-            pltpu.VMEM((PIECES, 2 * YN * PROWS, FEAT), BF),
-            pltpu.VMEM((PIECES, 2 * YN * PROWS, FEAT), BF),
-            pltpu.VMEM((PIECES, 2 * YN * PROWS, FEAT), BF),
-            pltpu.VMEM((n_y, 6 * PROWS, FEAT), BF),
-            pltpu.VMEM((n_y, PROWS, FEAT), BF),
-            pltpu.VMEM((n_x, 3 * PROWS, FEAT), BF),
-            pltpu.VMEM((n_x, YN * PROWS, FEAT), BF),
+            pltpu.VMEM((PIECES, CHUNKS, TILE, FEAT), BF),
+            pltpu.VMEM((n_y, 6 * PT, TILE, FEAT), BF),
+            pltpu.VMEM((n_y, PT, TILE, FEAT), BF),
+            pltpu.VMEM((n_x, 3 * PT, TILE, FEAT), BF),
+            pltpu.VMEM((n_x, YN * PT, TILE, FEAT), BF),
             pltpu.SMEM((ENDS,), jnp.int32),
             pltpu.SemaphoreType.DMA((copies,)),
             pltpu.SemaphoreType.DMA((copies,)),
@@ -380,7 +384,7 @@
         ),
         cost_estimate=pl.CostEstimate(flops=9 * 10**9, bytes_accessed=4 * MIB, transcendentals=0),
         name="graph_layer",
-    )(tile_row, tile_col, tile_count, features, weight, edge_row.T, edge_col.T, edge_weight.T)
+    )(tile_row, tile_col, tile_count, features, weight, edge_row.T, edge_col.T, edge_weight.T).reshape(NODE, FEAT)
 
 
 def solution(mesh):

time: 120 us -> 118 us (0.983)
    pallas_call x1, Pallas kernels: 117 us -> 116 us  [local(): pl.pallas_call(layer_kernel, out_shape=jax.ShapeDtypeStruct((NT, TILE, FE...]
where the time goes in v3:
time: 118 us
  Pallas kernels  116 us (98%)
  local copies, waits for them, and re-layouts  1.87 us (2%)
    pallas_call x1, Pallas kernels, local(): pl.pallas_call(layer_kernel, out_shape=jax.ShapeDtypeStruct((NT, TILE, FE...  116 us

profile of v3, /device:TPU:1, one launch (start us, length us, event | category | flops | bytes accessed | tf_op | source)
XLA Modules:
  0.0 118.2 jit_solution(13853883958604380032)
XLA Ops:
  0.7 115.7 %graph_layer.1 = bf16[16,128,128]{2,1,0:T(8,128)(2,1)} custom-call(s32[1024]{0:T(1024)} %tile_row.1, s32[1024]{0:T(1024)} %tile_col.1, s32[1]{0:T(128)S(6)} %copy.10.count_ref, bf16[2048,128]{1,0:T(8,128)(2,1)} %feat.1, bf16[128,128]{1,0:T(8,128)(2,1)} %weight.1, s32[64,1024]{1,0:T(8,128)} %bitcast.5, s32[64,1024]{1,0:T(8,128)} %bitcast.6, ...), custom_call_target="tpu_custom_call" | custom-call | flops 8999999488 | bytes 4194304 | tf_op jit(solution)/shard_map/graph_layer/pallas_call | solution.py:361
  116.3 1.9 %copy.11 = bf16[2048,128]{1,0:T(8,128)(2,1)} copy(bf16[2048,128]{1,0:T(8,128)(2,1)} %bitcast.4) | data formatting | bytes 1048576

commit v4 on v3

--- a/solution.py
+++ b/solution.py
@@ -20,6 +20,8 @@
 EARLY = 7
 LATE = NT - EARLY
 HALVES = {1: (EARLY, LATE // 2), -1: (EARLY + LATE // 2, LATE - LATE // 2)}
+BUILDS, BISECTS = 11, 7
+SERVICES = ((1, "late"), (1, "early"), (2, "late"), (1, "pair"), (2, "early"), (3, "late"), (2, "pair"), (4, "late"), (3, "early"), (3, "pair"))
 PIECES = 8
 PT = NT // PIECES
 CHUNKS = 2 * YN * PT
@@ -191,24 +193,21 @@
     for d in (1, -1):
         hops[1, d, "pair"] = ring(d, 1, *pair_early)
     final = []
-    for hop in (1, 2, 3):
-        for name, part in (("late", late), ("early", early), ("pair", pair_early)):
-            build_some(12)
-            bisect_some(8)
-            for d in (1, -1):
-                hops[hop, d, name].wait_recv()
-                if hop < 3:
-                    hops[hop + 1, d, name] = ring(d, hop + 1, *part)
-                elif name == "late":
-                    hops[4, d, name] = ring(d, 4, xlo, *HALVES[d])
-                elif (name == "early") == (d == 1):
-                    final.append(ring(d, 4, *part))
-                if name == "late":
-                    crossed.append(cross(d, hop, EARLY, LATE))
+    parts = {"late": late, "early": early, "pair": pair_early}
+    for hop, name in SERVICES:
+        build_some(BUILDS)
+        bisect_some(BISECTS)
+        for d in (1, -1):
+            hops[hop, d, name].wait_recv()
+            if hop < 3:
+                hops[hop + 1, d, name] = ring(d, hop + 1, *parts[name])
+            elif hop == 3 and name == "late":
+                hops[4, d, name] = ring(d, 4, xlo, *HALVES[d])
+            elif (name == "early") == (d == 1) and name != "late":
+                final.append(ring(d, 4, *parts[name]))
+            if name == "late":
+                crossed.append(cross(d, hop, *((EARLY, LATE) if hop < 4 else HALVES[d])))
     build_some(HALF // GROUP - built[0])
-    for d in (1, -1):
-        hops[4, d, "late"].wait_recv()
-        crossed.append(cross(d, 4, *HALVES[d]))
     for copy in final + crossed:
         copy.wait_recv()
 

time: 118 us -> 118 us (level)
  no operation moved by 1% of the time
where the time goes in v4:
time: 118 us
  Pallas kernels  115 us (97%)
  local copies, waits for them, and re-layouts  1.87 us (2%)
    pallas_call x1, Pallas kernels, local(): pl.pallas_call(layer_kernel, out_shape=jax.ShapeDtypeStruct((NT, TILE, FE...  115 us

profile of v4, /device:TPU:1, one launch (start us, length us, event | category | flops | bytes accessed | tf_op | source)
XLA Modules:
  0.0 117.8 jit_solution(11151971266993264692)
XLA Ops:
  0.7 115.3 %graph_layer.1 = bf16[16,128,128]{2,1,0:T(8,128)(2,1)} custom-call(s32[1024]{0:T(1024)} %tile_row.1, s32[1024]{0:T(1024)} %tile_col.1, s32[1]{0:T(128)S(6)} %copy.10.count_ref, bf16[2048,128]{1,0:T(8,128)(2,1)} %feat.1, bf16[128,128]{1,0:T(8,128)(2,1)} %weight.1, s32[64,1024]{1,0:T(8,128)} %bitcast.5, s32[64,1024]{1,0:T(8,128)} %bitcast.6, ...), custom_call_target="tpu_custom_call" | custom-call | flops 8999999488 | bytes 4194304 | tf_op jit(solution)/shard_map/graph_layer/pallas_call | solution.py:360
  115.9 1.9 %copy.11 = bf16[2048,128]{1,0:T(8,128)(2,1)} copy(bf16[2048,128]{1,0:T(8,128)(2,1)} %bitcast.4) | data formatting | bytes 1048576

commit v5 on v4

--- a/solution.py
+++ b/solution.py
@@ -20,7 +20,7 @@
 EARLY = 7
 LATE = NT - EARLY
 HALVES = {1: (EARLY, LATE // 2), -1: (EARLY + LATE // 2, LATE - LATE // 2)}
-BUILDS, BISECTS = 11, 7
+BUILDS, BISECTS = 9, 7
 SERVICES = ((1, "late"), (1, "early"), (2, "late"), (1, "pair"), (2, "early"), (3, "late"), (2, "pair"), (4, "late"), (3, "early"), (3, "pair"))
 PIECES = 8
 PT = NT // PIECES
@@ -188,7 +188,7 @@
         hops[1, d, "early"] = ring(d, 1, *early)
     crossed = [cross(1, 0, EARLY, LATE)]
     lax.fori_loop(0, HALF // 128, prep, 0)
-    build_some(8)
+    build_some(20)
     cross_early.wait_recv()
     for d in (1, -1):
         hops[1, d, "pair"] = ring(d, 1, *pair_early)

time: 118 us -> 118 us (level)
  no operation moved by 1% of the time
where the time goes in v5:
time: 118 us
  Pallas kernels  116 us (98%)
  local copies, waits for them, and re-layouts  1.87 us (2%)
    pallas_call x1, Pallas kernels, local(): pl.pallas_call(layer_kernel, out_shape=jax.ShapeDtypeStruct((NT, TILE, FE...  116 us

profile of v5, /device:TPU:1, one launch (start us, length us, event | category | flops | bytes accessed | tf_op | source)
XLA Modules:
  0.0 118.2 jit_solution(14346721941511729669)
XLA Ops:
  0.7 115.6 %graph_layer.1 = bf16[16,128,128]{2,1,0:T(8,128)(2,1)} custom-call(s32[1024]{0:T(1024)} %tile_row.1, s32[1024]{0:T(1024)} %tile_col.1, s32[1]{0:T(128)S(6)} %copy.10.count_ref, bf16[2048,128]{1,0:T(8,128)(2,1)} %feat.1, bf16[128,128]{1,0:T(8,128)(2,1)} %weight.1, s32[64,1024]{1,0:T(8,128)} %bitcast.5, s32[64,1024]{1,0:T(8,128)} %bitcast.6, ...), custom_call_target="tpu_custom_call" | custom-call | flops 8999999488 | bytes 4194304 | tf_op jit(solution)/shard_map/graph_layer/pallas_call | solution.py:360
  116.3 1.9 %copy.11 = bf16[2048,128]{1,0:T(8,128)(2,1)} copy(bf16[2048,128]{1,0:T(8,128)(2,1)} %bitcast.4) | data formatting | bytes 1048576
